TPU v7x, 128 devices: a whole 4x4x4 slice. The times are simulated.
128 devices in a mesh: seq: 16 (over z, x), head: 8 (over y, core).
Axes of the slice: x: 4, y: 4, z: 4, core: 2. Of those that a mesh axis runs over, the one named last changes fastest.
Arguments:
- queries: float32 [16384, 4096], P('seq', 'head'), may hold values from -6 to 6
- keys: float32 [16384, 4096], P('seq', 'head'), may hold values from -6 to 6
- values: float32 [16384, 4096], P('seq', 'head'), may hold values from -6 to 6
- out_grad: float32 [16384, 4096], P('seq', 'head'), may hold values from -6 to 6
- inputs: float32 [16384, 4096], P('seq', 'head'), may hold values from -20 to 20
- row_state: float32 [8, 4096], P('head', 'seq'), may hold values from 0.2 to 5
- col_state: float32 [16, 4096], P('seq', 'head'), may hold values from 0.2 to 5
Outputs:
- query_grad: float32 [16384, 4096], P('seq', 'head')
- key_grad: float32 [16384, 4096], P('seq', 'head')
- update: float32 [4096, 4096], P('seq', 'head')
- row_next: float32 [8, 4096], P('head', 'seq')
- col_next: float32 [16, 4096], P('seq', 'head')
All inputs are finite; a program needn't handle non-finite values.
Results may differ from a plain program's by a relative error of at most 0.0001.
Values sent between devices are 32-bit elements; how exact they have to be, the bound alone decides.
A program may use at most 128 MiB of HBM per device.

v0:
```python
import functools

import jax
import jax.numpy as jnp
import numpy as np
from jax import lax
from jax.experimental import pallas as pl
from jax.experimental.pallas import tpu as pltpu
from jax.sharding import PartitionSpec as P

F32 = jnp.float32
BF16 = jnp.bfloat16
MESH = pl.DeviceIdType.MESH

HEAD_DIM = 128
TOK = 1024
HEADS = 4
CH = 256
NCH = TOK // CH
HALF = 256
MOMENT_EPS = 1e-06
DECAY = 0.9
ATTN_SCALE = float(np.float32(1.0) / np.sqrt(np.float32(128 * 16384)))

NN = (((1,), (0,)), ((), ()))
NT = (((1,), (1,)), ((), ()))

SLOT_DY = (3, 1, 2, 0)
JOBS = ((3, 0), (3, 1), (0, 0), (1, 1), (0, 1), (1, 0), (2, 0), (2, 1))


def dot(a, b, dims=NN):
    return lax.dot_general(a, b, dims, preferred_element_type=F32)


def split(a):
    hi = a.astype(BF16)
    lo = (a - hi.astype(F32)).astype(BF16)
    return hi, lo


def mm_nt(a, b):
    both = jnp.concatenate([a[0], a[1]], axis=1)
    twice = jnp.concatenate([b[0], b[0]], axis=1)
    return dot(both, twice, NT) + dot(a[0], b[1], NT)


def mm_nn(a, b):
    wide = jnp.concatenate([b[0], b[1]], axis=1)
    first = dot(a[0], wide)
    return first[:, :128] + first[:, 128:] + dot(a[1], b[0])


def mm_state(a, b):
    both = jnp.concatenate([a[0], a[1]], axis=1)
    wide = jnp.concatenate([b[0], b[1]], axis=1)
    out = dot(both, jnp.concatenate([wide, wide], axis=0))
    return out[:, :128] + out[:, 128:]


def mm3(a, b):
    return dot(a[0], b[0]) + dot(a[0], b[1]) + dot(a[1], b[0])


def kernel(
    q_hbm, k_hbm, v_hbm, g_hbm, x_hbm, rowst, colst,
    qg_hbm, kg_hbm, upd, rown, coln,
    io, qg, kg, vt, vthi, vtlo, xbuf, xhi, xlo,
    rev_c, fwd_c, tot, ex1, val, tz, ex2, enter, run,
    pbuf, rs1, rs2, rs3, rs4, wfin,
    ld_sem, xo_sem, xs_sem, xr_sem, es_sem, er_sem, vs_sem, vr_sem,
    rss_sem, rsr_sem, fs_sem, fr_sem, out_sem,
):
    sq = lax.axis_index("seq")
    hd = lax.axis_index("head")
    z, x = sq // 4, sq % 4
    y, c = hd // 2, hd % 2

    def at_x(d):
        return (z * 4 + (x + d) % 4, hd)

    def at_z(d):
        return (((z + d) % 4) * 4 + x, hd)

    def at_y(d):
        return (sq, ((y + d) % 4) * 2 + c)

    sibling = (sq, y * 2 + 1 - c)

    def remote(src, dst, send, recv, dev):
        return pltpu.make_async_remote_copy(
            src_ref=src, dst_ref=dst, send_sem=send, recv_sem=recv, device_id=dev, device_id_type=MESH
        )

    def load(n, h):
        src = (q_hbm, k_hbm, v_hbm, g_hbm)[n]
        return pltpu.make_async_copy(
            src.at[:, pl.ds(h * 128, 128)], io.at[n, h], ld_sem.at[n, h]
        )

    for n in (3, 0, 2, 1):
        for h in range(HEADS):
            load(n, h).start()

    barrier = pltpu.get_barrier_semaphore()

    def greet(dev):
        pl.semaphore_signal(barrier, inc=1, device_id=dev, device_id_type=MESH)

    for dev in (at_y(1), at_y(3), sibling):
        greet(dev)
    for d in (1, 2, 3):
        greet(at_x(d))
        greet(at_z(d))
    for zs in range(4):

        @pl.when(jnp.logical_or(z != zs, z != y))
        def _(zs=zs):
            greet((zs * 4 + x, z * 2 + c))

    pl.semaphore_wait(barrier, 12 + (z != y).astype(jnp.int32))

    cols = (pl.ds(0, HALF), pl.ds(HALF, HALF))
    x_up = [
        remote(x_hbm.at[:, cols[i]], xbuf.at[0, :, cols[i]], xs_sem.at[0, i], xr_sem.at[0, i], at_y(1))
        for i in (0, 1)
    ]
    x_down = [
        remote(x_hbm.at[:, cols[i]], xbuf.at[1, :, cols[i]], xs_sem.at[1, i], xr_sem.at[1, i], at_y(3))
        for i in (0, 1)
    ]
    x_up[0].start()
    x_down[1].start()
    x_up[1].start()
    x_down[0].start()
    x_fwd_up = remote(
        xbuf.at[0, :, cols[0]], xbuf.at[2, :, cols[0]], xs_sem.at[2, 0], xr_sem.at[2, 0], at_y(1)
    )
    x_fwd_down = remote(
        xbuf.at[1, :, cols[1]], xbuf.at[2, :, cols[1]], xs_sem.at[2, 1], xr_sem.at[2, 1], at_y(3)
    )
    x_own = pltpu.make_async_copy(x_hbm, xbuf.at[3], xo_sem)
    x_own.start()

    def ex_a(st, d):
        dst = (x + d) % 4
        return remote(tot.at[st, dst], ex1.at[st, d - 1], es_sem.at[st, 0, d - 1], er_sem.at[st, 0, d - 1], at_x(d))

    def ex_b(st, d):
        return remote(tz.at[st], ex2.at[st, d - 1], es_sem.at[st, 1, d - 1], er_sem.at[st, 1, d - 1], at_z(d))

    def ex_c(st, d):
        return remote(val.at[st, d], enter.at[st, x], es_sem.at[st, 2, d - 1], er_sem.at[st, 2, d - 1], at_x(d))

    def counts(st, source, target):
        reached = source > target if st == 0 else source < target
        return reached.astype(F32)

    def send_a(st):
        for d in (1, 2, 3):
            ex_a(st, d).start()

    def send_b(st):
        for d in (1, 2, 3):
            ex_a(st, d).wait_recv()
        parts = [tot[st, x]] + [ex1[st, d - 1] for d in (1, 2, 3)]
        tz[st] = parts[0] + parts[1] + parts[2] + parts[3]
        for d in (1, 2, 3):
            ex_b(st, d).start()
        for e in range(4):
            target = (x + e) % 4
            terms = [counts(st, (x + 4 - d) % 4, target) * parts[d] for d in range(4)]
            val[st, e] = terms[0] + terms[1] + terms[2] + terms[3]

    def send_c(st):
        for d in (1, 2, 3):
            ex_b(st, d).wait_recv()
        base = sum(counts(st, (z + 4 - d) % 4, z) * ex2[st, d - 1] for d in (1, 2, 3))
        for e in (1, 2, 3):
            val[st, e] = val[st, e] + base
            ex_c(st, e).start()
        enter[st, x] = val[st, 0] + base

    def recv_c(st):
        for d in (1, 2, 3):
            remote(
                val.at[st, d], enter.at[st, (x + 4 - d) % 4],
                es_sem.at[st, 2, d - 1], er_sem.at[st, 2, d - 1], at_x(d),
            ).wait_recv()

    def rows(ch):
        return pl.ds(pl.multiple_of(ch * CH, CH), CH)

    def rev_states(h, carry):
        load(3, h).wait()
        load(0, h).wait()
        total = jnp.zeros((128, 128), F32)
        for ch in range(NCH):
            gt = split(io[3, h, ch * CH : (ch + 1) * CH].T)
            part = mm_nn(gt, split(io[0, h, ch * CH : (ch + 1) * CH]))
            rev_c[h, ch] = part
            total = total + part
        tot[0, h] = total
        return carry

    def fwd_states(h, carry):
        load(2, h).wait()
        load(1, h).wait()
        total = jnp.zeros((128, 128), F32)
        for ch in range(NCH):
            vtr = split(io[2, h, ch * CH : (ch + 1) * CH].T)
            part = mm_nn(vtr, split(io[1, h, ch * CH : (ch + 1) * CH]))
            fwd_c[h, ch] = part
            total = total + part
        tot[1, h] = total
        return carry

    lax.fori_loop(0, HEADS, rev_states, 0)
    send_a(0)
    lax.fori_loop(0, HEADS, fwd_states, 0)
    send_a(1)

    row_at = lax.broadcasted_iota(jnp.int32, (CH, CH), 0)
    col_at = lax.broadcasted_iota(jnp.int32, (CH, CH), 1)

    def intra(i, carry):
        h, ch = i // NCH, i % NCH
        for when, step in ((2, functools.partial(send_b, 0)), (4, functools.partial(send_b, 1)),
                           (6, functools.partial(send_c, 0)), (8, functools.partial(send_c, 1))):
            pl.when(i == when)(step)
        qf, kf, vf, gf = (io[n, h, rows(ch)] for n in range(4))
        q, k, v, g = split(qf), split(kf), split(vf), split(gf)
        causal = col_at <= row_at
        gv = split(jnp.where(causal, mm_nt(g, v), 0.0))
        qg[h, rows(ch)] = mm_nn(gv, k)
        vg = split(jnp.where(row_at <= col_at, mm_nt(v, g), 0.0))
        kg[h, rows(ch)] = mm_nn(vg, q)
        qk = split(jnp.where(causal, mm_nt(q, k), 0.0))
        vt[c * HEADS + h, :, rows(ch)] = mm3(split(gf.T), qk)
        return carry

    lax.fori_loop(0, HEADS * NCH, intra, 0)

    recv_c(0)

    def vt_copy(h):
        at = c * HEADS + h
        return remote(vt.at[at], vt.at[at], vs_sem.at[h], vr_sem.at[h], sibling)

    def finish_values(h, carry):
        suffix = enter[0, h]
        at = c * HEADS + h
        for ch in reversed(range(NCH)):
            span = pl.ds(ch * CH, CH)
            more = mm_nt(split(suffix), split(io[1, h, span]))
            done = ATTN_SCALE * (vt[at, :, span] + more)
            vt[at, :, span] = done
            hi, lo = split(done)
            vthi[at, :, span] = hi
            vtlo[at, :, span] = lo
            suffix = suffix + rev_c[h, ch]
        vt_copy(h).start()
        return carry

    lax.fori_loop(0, HEADS, finish_values, 0)
    recv_c(1)

    def out_copy(n, h):
        dst = (qg_hbm, kg_hbm)[n]
        return pltpu.make_async_copy((qg, kg)[n].at[h], dst.at[:, pl.ds(h * 128, 128)], out_sem.at[n, h])

    def finish_keys(h):
        suffix = enter[0, h]
        for ch in reversed(range(NCH)):
            span = pl.ds(ch * CH, CH)
            kg[h, span] = ATTN_SCALE * (kg[h, span] + mm_state(split(io[2, h, span]), split(suffix)))
            suffix = suffix + rev_c[h, ch]

    def finish_queries(h):
        prefix = enter[1, h]
        for ch in range(NCH):
            span = pl.ds(ch * CH, CH)
            qg[h, span] = ATTN_SCALE * (qg[h, span] + mm_state(split(io[3, h, span]), split(prefix)))
            prefix = prefix + fwd_c[h, ch]

    def finish_rest(h, carry):
        finish_keys(h)
        finish_queries(h)
        return carry

    lax.fori_loop(0, HEADS, finish_rest, 0)
    for n in (0, 1):
        for h in range(HEADS):
            out_copy(n, h).start()

    def take_values(h, carry):
        at = (1 - c) * HEADS + h
        remote(vt.at[at], vt.at[at], vs_sem.at[h], vr_sem.at[h], sibling).wait_recv()
        hi, lo = split(vt[at])
        vthi[at] = hi
        vtlo[at] = lo
        return carry

    lax.fori_loop(0, HEADS, take_values, 0)

    def product(j):
        slot, half = JOBS[j]

        def cut(t, carry):
            hi, lo = split(xbuf[slot, rows(t), cols[half]])
            xhi[rows(t)] = hi
            xlo[rows(t)] = lo
            return carry

        lax.fori_loop(0, TOK // CH, cut, 0)

        def block(a, carry):
            left = (vthi[pl.ds(2 * a, 2)].reshape(256, TOK), vtlo[pl.ds(2 * a, 2)].reshape(256, TOK))
            out = mm3(left, (xhi[...], xlo[...])).reshape(4, 64, HALF)
            if half == 0:
                pbuf[j, a] = out
            else:
                for r in range(4):
                    pbuf[j, r, a] = out[r]
            return carry

        lax.fori_loop(0, 4, block, 0)

    first = ((x, at_x), (z, at_z))
    second = ((z, at_z), (x, at_x))

    def rs(j, n, src, dst, dev):
        return remote(src, dst, rss_sem.at[j, n], rsr_sem.at[j, n], dev)

    def ring1(j):
        m, at = first[JOBS[j][1]]
        far = (m + 2) % 4
        return (
            rs(j, 0, pbuf.at[j, far, 0:2], rs1.at[j, 0], at(1)),
            rs(j, 1, pbuf.at[j, far, 2:4], rs1.at[j, 1], at(3)),
        )

    def ring2(j):
        m, at = first[JOBS[j][1]]
        return (
            rs(j, 2, pbuf.at[j, (m + 1) % 4], rs2.at[j, 0], at(1)),
            rs(j, 3, pbuf.at[j, (m + 3) % 4], rs2.at[j, 1], at(3)),
        )

    def ring3(j):
        m, _ = first[JOBS[j][1]]
        n, at = second[JOBS[j][1]]
        far = (n + 2) % 4
        return (
            rs(j, 4, pbuf.at[j, m, far, 0:32], rs3.at[j, 0], at(1)),
            rs(j, 5, pbuf.at[j, m, far, 32:64], rs3.at[j, 1], at(3)),
        )

    def ring4(j):
        m, _ = first[JOBS[j][1]]
        n, at = second[JOBS[j][1]]
        return (
            rs(j, 6, pbuf.at[j, m, (n + 1) % 4], rs4.at[j, 0], at(1)),
            rs(j, 7, pbuf.at[j, m, (n + 3) % 4], rs4.at[j, 1], at(3)),
        )

    def final(j):
        slot, half = JOBS[j]
        m, _ = first[half]
        n, _ = second[half]
        target = (y + SLOT_DY[slot]) % 4
        return remote(
            pbuf.at[j, m, n], wfin.at[z, :, cols[half]], fs_sem.at[j], fr_sem.at[z, half],
            (y * 4 + x, target * 2 + c),
        )

    def stage1(j):
        for copy in ring1(j):
            copy.start()

    def stage2(j):
        m, _ = first[JOBS[j][1]]
        got, send = ring1(j), ring2(j)
        got[0].wait_recv()
        up = (m + 1) % 4
        pbuf[j, up, 0:2] = pbuf[j, up, 0:2] + rs1[j, 0]
        send[0].start()
        got[1].wait_recv()
        down = (m + 3) % 4
        pbuf[j, down, 2:4] = pbuf[j, down, 2:4] + rs1[j, 1]
        send[1].start()

    def stage3(j):
        m, _ = first[JOBS[j][1]]
        for copy in ring2(j):
            copy.wait_recv()
        pbuf[j, m] = pbuf[j, m] + (rs2[j, 0] + rs2[j, 1])
        for copy in ring3(j):
            copy.start()

    def stage4(j):
        m, _ = first[JOBS[j][1]]
        n, _ = second[JOBS[j][1]]
        got, send = ring3(j), ring4(j)
        got[0].wait_recv()
        up = (n + 1) % 4
        pbuf[j, m, up, 0:32] = pbuf[j, m, up, 0:32] + rs3[j, 0]
        send[0].start()
        got[1].wait_recv()
        down = (n + 3) % 4
        pbuf[j, m, down, 32:64] = pbuf[j, m, down, 32:64] + rs3[j, 1]
        send[1].start()

    def stage5(j):
        slot, half = JOBS[j]
        m, _ = first[half]
        n, _ = second[half]
        for copy in ring4(j):
            copy.wait_recv()
        pbuf[j, m, n] = pbuf[j, m, n] + (rs4[j, 0] + rs4[j, 1])
        if slot == 3:

            @pl.when(z != y)
            def _():
                final(j).start()

            @pl.when(z == y)
            def _():
                wfin[z, :, cols[half]] = pbuf[j, m, n]
        else:
            final(j).start()

    stages = (stage1, stage2, stage3, stage4, stage5)

    def arrive(j):
        slot, half = JOBS[j]
        if slot == 3:
            if half == 0:
                x_own.wait()
        elif slot == 0:
            x_up[half].wait_recv()
            if half == 0:
                x_fwd_up.start()
        elif slot == 1:
            x_down[half].wait_recv()
            if half == 1:
                x_fwd_down.start()
        else:
            (x_fwd_up, x_fwd_down)[half].wait_recv()

    def advance(jobs, extra):
        pending = []
        for step in range(len(jobs) + extra):
            if step < len(jobs):
                arrive(jobs[step])
                product(jobs[step])
                pending.append([jobs[step], 0])
            for item in reversed(pending):
                if item[1] < len(stages):
                    stages[item[1]](item[0])
                    item[1] += 1

    advance((0, 1, 2, 3, 4, 5), 4)
    advance((6, 7), 4)

    for half in (0, 1):
        for zs in range(4):

            @pl.when(jnp.logical_or(z != zs, z != y))
            def _(half=half, zs=zs):
                remote(
                    pbuf.at[0, 0, 0], wfin.at[zs, :, cols[half]], fs_sem.at[0], fr_sem.at[zs, half], sibling
                ).wait_recv()

    w = wfin[...].reshape(256, 512) / jnp.sqrt(F32(16384.0))
    squares = w * w + MOMENT_EPS
    row_mean = jnp.broadcast_to(jnp.mean(squares, axis=1, keepdims=True), (256, 128))
    col_mean = jnp.mean(squares, axis=0, keepdims=True)
    row_old = jnp.broadcast_to(rowst[...], (128, 256)).T
    row_new = DECAY * row_old + (1.0 - DECAY) * row_mean
    col_new = DECAY * colst[...] + (1.0 - DECAY) * col_mean
    rown[...] = row_new.T[0:1]
    coln[...] = col_new
    row_one = row_new[:, 0:1]
    average = jnp.mean(row_one, axis=0, keepdims=True)
    upd[...] = w * lax.rsqrt(row_one * col_new / average)

    for n in (0, 1):
        for h in range(HEADS):
            out_copy(n, h).wait()
    for st in (0, 1):
        for d in (1, 2, 3):
            ex_a(st, d).wait_send()
            ex_b(st, d).wait_send()
            ex_c(st, d).wait_send()
    for h in range(HEADS):
        vt_copy(h).wait_send()
    for copy in (*x_up, *x_down, x_fwd_up, x_fwd_down):
        copy.wait_send()
    for j in range(len(JOBS)):
        for ring in (ring1, ring2, ring3, ring4):
            for copy in ring(j):
                copy.wait_send()
        if JOBS[j][0] == 3:

            @pl.when(z != y)
            def _(j=j):
                final(j).wait_send()
        else:
            final(j).wait_send()


def shards(queries, keys, values, out_grad, inputs, row_state, col_state):
    hbm = pl.BlockSpec(memory_space=pl.ANY)
    vmem = pl.BlockSpec(memory_space=pltpu.VMEM)
    jobs = len(JOBS)
    dma = pltpu.SemaphoreType.DMA
    scratch = [
        pltpu.VMEM((4, HEADS, TOK, 128), F32),
        pltpu.VMEM((HEADS, TOK, 128), F32),
        pltpu.VMEM((HEADS, TOK, 128), F32),
        pltpu.VMEM((2 * HEADS, 128, TOK), F32),
        pltpu.VMEM((2 * HEADS, 128, TOK), BF16),
        pltpu.VMEM((2 * HEADS, 128, TOK), BF16),
        pltpu.VMEM((4, TOK, 512), F32),
        pltpu.VMEM((TOK, HALF), BF16),
        pltpu.VMEM((TOK, HALF), BF16),
        pltpu.VMEM((HEADS, NCH, 128, 128), F32),
        pltpu.VMEM((HEADS, NCH, 128, 128), F32),
        pltpu.VMEM((2, HEADS, 128, 128), F32),
        pltpu.VMEM((2, 3, 128, 128), F32),
        pltpu.VMEM((2, 4, 128, 128), F32),
        pltpu.VMEM((2, 128, 128), F32),
        pltpu.VMEM((2, 3, 128, 128), F32),
        pltpu.VMEM((2, HEADS, 128, 128), F32),
        pltpu.VMEM((8, 128), F32),
        pltpu.VMEM((jobs, 4, 4, 64, HALF), F32),
        pltpu.VMEM((jobs, 2, 2, 64, HALF), F32),
        pltpu.VMEM((jobs, 2, 4, 64, HALF), F32),
        pltpu.VMEM((jobs, 2, 32, HALF), F32),
        pltpu.VMEM((jobs, 2, 64, HALF), F32),
        pltpu.VMEM((4, 64, 512), F32),
        dma((4, HEADS)),
        dma,
        dma((3, 2)),
        dma((3, 2)),
        dma((2, 3, 3)),
        dma((2, 3, 3)),
        dma((HEADS,)),
        dma((HEADS,)),
        dma((jobs, 8)),
        dma((jobs, 8)),
        dma((jobs,)),
        dma((4, 2)),
        dma((2, HEADS)),
    ]
    return pl.pallas_call(
        kernel,
        out_shape=(
            jax.ShapeDtypeStruct((TOK, 512), F32),
            jax.ShapeDtypeStruct((TOK, 512), F32),
            jax.ShapeDtypeStruct((256, 512), F32),
            jax.ShapeDtypeStruct((1, 256), F32),
            jax.ShapeDtypeStruct((1, 512), F32),
        ),
        in_specs=[hbm] * 5 + [vmem] * 2,
        out_specs=(hbm, hbm, vmem, vmem, vmem),
        scratch_shapes=scratch,
        compiler_params=pltpu.CompilerParams(
            collective_id=0, has_side_effects=True, vmem_limit_bytes=60 * 1024 * 1024
        ),
        cost_estimate=pl.CostEstimate(flops=20_000_000_000, bytes_accessed=16_000_000, transcendentals=0),
    )(queries, keys, values, out_grad, inputs, row_state, col_state)


def solution(mesh):
    in_specs = (
        P("seq", "head"),
        P("seq", "head"),
        P("seq", "head"),
        P("seq", "head"),
        P("seq", "head"),
        P("head", "seq"),
        P("seq", "head"),
    )
    out_specs = (
        P("seq", "head"),
        P("seq", "head"),
        P("seq", "head"),
        P("head", "seq"),
        P("seq", "head"),
    )
    return jax.shard_map(shards, mesh=mesh, in_specs=in_specs, out_specs=out_specs, check_vma=False)
```

profile of v0, /device:TPU:104, one launch (start us, length us, event | category | flops | bytes accessed | tf_op | source)
XLA Modules:
  0.0 124.3 jit_solution(6542793802103299518)
XLA Ops:
  0.6 117.1 %shard_map.110 = (f32[1024,512]{1,0:T(8,128)}, f32[1024,512]{1,0:T(8,128)}, f32[256,512]{1,0:T(8,128)}, f32[1,256]{1,0:T(1,128)}, f32[1,512]{1,0:T(1,128)}) custom-call(f32[1024,512]{1,0:T(8,128)} %q_hbm.1, f32[1024,512]{1,0:T(8,128)} %k_hbm.1, f32[1024,512]{1,0:T(8,128)} %v_hbm.1, f32[1024,512]{1,0:T(8,128)} %g_hbm.1, f32[1024,512]{1,0:T(8,128)} %x_hbm.1, ...), custom_call_target="tpu_custom_call" | custom-call | flops 20000000000 | bytes 16000000 | tf_op jit(solution)/shard_map/pallas_call | solution.py:557
  117.7 0.0 copy-start
  117.7 3.2 %copy.17 = f32[1024,512]{1,0:T(8,128)} copy(f32[1024,512]{1,0:T(8,128)} %get-tuple-element.10) | data formatting | bytes 4194304
  120.9 0.0 copy-done
  120.9 0.0 copy-start.1
  120.9 0.0 copy-start.3
  121.0 0.0 copy-start.2
  121.0 1.3 %copy.18 = f32[1024,512]{1,0:T(8,128)} copy(f32[1024,512]{1,0:T(8,128)S(1)} %copy-done) | data formatting | bytes 4194304
  122.3 0.0 copy-done.1
  122.3 0.8 copy.19
  123.1 0.0 copy-done.3
  123.1 0.6 copy.20
  123.7 0.0 copy-done.2
  123.7 0.6 copy.21
Async XLA Ops:
  117.7 3.2 %copy-start = (f32[1024,512]{1,0:T(8,128)S(1)}, f32[1024,512]{1,0:T(8,128)}, u32[]{:S(2)}) copy-start(f32[1024,512]{1,0:T(8,128)} %get-tuple-element.11) | copy-start | bytes 6291460
  120.9 1.4 %copy-start.1 = (f32[256,512]{1,0:T(8,128)S(1)}, f32[256,512]{1,0:T(8,128)}, u32[]{:S(2)}) copy-start(f32[256,512]{1,0:T(8,128)} %get-tuple-element.12) | copy-start | bytes 1572868
  120.9 2.2 %copy-start.3 = (f32[1,256]{1,0:T(1,128)S(1)}, f32[1,256]{1,0:T(1,128)}, u32[]{:S(2)}) copy-start(f32[1,256]{1,0:T(1,128)} %get-tuple-element.13) | copy-start | bytes 3076
  121.0 2.7 %copy-start.2 = (f32[1,512]{1,0:T(1,128)S(1)}, f32[1,512]{1,0:T(1,128)}, u32[]{:S(2)}) copy-start(f32[1,512]{1,0:T(1,128)} %get-tuple-element.14) | copy-start | bytes 6148
where the time goes:
time: 126 us; the launch traced here: 124 us
  Pallas kernels  117 us (93%)
  local copies, waits for them, and re-layouts  6.54 us (5%)
    pallas_call x1, Pallas kernels, shards(): pl.pallas_call(kernel, out_shape=(jax.ShapeDtypeStruct((TOK, 512), F32),...  117 us
    unnamed x13, local copies, waits for them, and re-layouts  6.54 us

commit v1 on v0

v1 whole, which is shorter than its diff:
```python
import jax
import jax.numpy as jnp
import numpy as np
from jax import lax
from jax.experimental import pallas as pl
from jax.experimental.pallas import tpu as pltpu
from jax.sharding import PartitionSpec as P

F32 = jnp.float32
BF16 = jnp.bfloat16
MESH = pl.DeviceIdType.MESH

HEAD_DIM = 128
TOK = 1024
HEADS = 4
CH = 256
NCH = TOK // CH
PART = 128
MOMENT_EPS = 1e-06
DECAY = 0.9
ATTN_SCALE = float(np.float32(1.0) / np.sqrt(np.float32(128 * 16384)))

NN = (((1,), (0,)), ((), ()))
NT = (((1,), (1,)), ((), ()))

SLOT_DY = (3, 1, 2, 0)
STEPS = ((3, 0), (3, 1), (0, 0), (1, 0), (0, 1), (1, 1), (2, 0), (2, 1))
JOBS = 2 * len(STEPS)


def dot(a, b, dims=NN):
    return lax.dot_general(a, b, dims, preferred_element_type=F32)


def split(a):
    hi = a.astype(BF16)
    lo = (a - hi.astype(F32)).astype(BF16)
    return hi, lo


def mm_nt(a, b):
    both = jnp.concatenate([a[0], a[1]], axis=1)
    twice = jnp.concatenate([b[0], b[0]], axis=1)
    return dot(both, twice, NT) + dot(a[0], b[1], NT)


def mm_nn(a, b):
    wide = jnp.concatenate([b[0], b[1]], axis=1)
    first = dot(a[0], wide)
    return first[:, :128] + first[:, 128:] + dot(a[1], b[0])


def mm_state(a, b):
    both = jnp.concatenate([a[0], a[1]], axis=1)
    wide = jnp.concatenate([b[0], b[1]], axis=1)
    out = dot(both, jnp.concatenate([wide, wide], axis=0))
    return out[:, :128] + out[:, 128:]


def mm3(a, b):
    return dot(a[0], b[0]) + dot(a[0], b[1]) + dot(a[1], b[0])


def kernel(
    q_hbm, k_hbm, v_hbm, g_hbm, x_hbm,
    qg_hbm, kg_hbm, w_out,
    io, qg, kg, vt, vthi, vtlo, xbuf, xhi, xlo,
    rev_c, fwd_c, tot, ex1, val, tz, ex2, enter,
    pbuf, rs1, rs2, rs3, wfin,
    ld_sem, xo_sem, xs_sem, xr_sem, xf_sem, xg_sem, es_sem, er_sem, vs_sem, vr_sem,
    rss_sem, rsr_sem, fs_sem, fr_sem, out_sem,
):
    sq = lax.axis_index("seq")
    hd = lax.axis_index("head")
    z, x = sq // 4, sq % 4
    y, c = hd // 2, hd % 2

    def at_x(d):
        return (z * 4 + (x + d) % 4, hd)

    def at_z(d):
        return (((z + d) % 4) * 4 + x, hd)

    def at_y(d):
        return (sq, ((y + d) % 4) * 2 + c)

    sibling = (sq, y * 2 + 1 - c)

    def remote(src, dst, send, recv, dev):
        return pltpu.make_async_remote_copy(
            src_ref=src, dst_ref=dst, send_sem=send, recv_sem=recv, device_id=dev, device_id_type=MESH
        )

    def load(n, h):
        src = (q_hbm, k_hbm, v_hbm, g_hbm)[n]
        return pltpu.make_async_copy(
            src.at[:, pl.ds(h * 128, 128)], io.at[n, h], ld_sem.at[n, h]
        )

    barrier = pltpu.get_barrier_semaphore()

    def greet(dev):
        pl.semaphore_signal(barrier, inc=1, device_id=dev, device_id_type=MESH)

    for dev in (at_y(1), at_y(3), sibling):
        greet(dev)
    for d in (1, 2, 3):
        greet(at_x(d))
        greet(at_z(d))
    for zs in range(4):

        @pl.when(jnp.logical_or(z != zs, z != y))
        def _(zs=zs):
            greet((zs * 4 + x, z * 2 + c))

    for n in (3, 0, 2, 1):
        for h in range(HEADS):
            load(n, h).start()

    pl.semaphore_wait(barrier, 12 + (z != y).astype(jnp.int32))

    def cols(half, part):
        return pl.ds(half * 256 + part * PART, PART)

    def x_direct(up, half, part):
        at = cols(half, part)
        slot = 0 if up else 1
        return remote(
            x_hbm.at[:, at], xbuf.at[slot, :, at], xs_sem.at[slot, half, part], xr_sem.at[slot, half, part],
            at_y(1 if up else 3),
        )

    def x_forward(half, part, tok):
        at = cols(half, part)
        span = pl.ds(tok * (TOK // 2), TOK // 2)
        sem = 2 * tok + part
        return remote(
            xbuf.at[half, span, at], xbuf.at[2, span, at], xf_sem.at[half, sem], xg_sem.at[half, sem],
            at_y(1 if half == 0 else 3),
        )

    def forward(part):
        x_direct(True, 0, part).wait_recv()
        x_direct(False, 1, part).wait_recv()
        for tok in (0, 1):
            x_forward(0, part, tok).start()
            x_forward(1, part, tok).start()

    for part in (0, 1):
        x_direct(True, 0, part).start()
        x_direct(False, 1, part).start()
        x_direct(True, 1, part).start()
        x_direct(False, 0, part).start()
    x_own = pltpu.make_async_copy(x_hbm, xbuf.at[3], xo_sem)
    x_own.start()

    def ex_a(st, d):
        dst = (x + d) % 4
        return remote(tot.at[st, dst], ex1.at[st, d - 1], es_sem.at[st, 0, d - 1], er_sem.at[st, 0, d - 1], at_x(d))

    def ex_b(st, d):
        return remote(tz.at[st], ex2.at[st, d - 1], es_sem.at[st, 1, d - 1], er_sem.at[st, 1, d - 1], at_z(d))

    def ex_c(st, d):
        return remote(val.at[st, d], enter.at[st, x], es_sem.at[st, 2, d - 1], er_sem.at[st, 2, d - 1], at_x(d))

    def counts(st, source, target):
        reached = source > target if st == 0 else source < target
        return reached.astype(F32)

    def send_a(st):
        for d in (1, 2, 3):
            ex_a(st, d).start()

    def send_b(st):
        for d in (1, 2, 3):
            ex_a(st, d).wait_recv()
        parts = [tot[st, x]] + [ex1[st, d - 1] for d in (1, 2, 3)]
        tz[st] = parts[0] + parts[1] + parts[2] + parts[3]
        for d in (1, 2, 3):
            ex_b(st, d).start()
        for e in range(4):
            target = (x + e) % 4
            terms = [counts(st, (x + 4 - d) % 4, target) * parts[d] for d in range(4)]
            val[st, e] = terms[0] + terms[1] + terms[2] + terms[3]

    def send_c(st):
        for d in (1, 2, 3):
            ex_b(st, d).wait_recv()
        base = sum(counts(st, (z + 4 - d) % 4, z) * ex2[st, d - 1] for d in (1, 2, 3))
        for e in (1, 2, 3):
            val[st, e] = val[st, e] + base
            ex_c(st, e).start()
        enter[st, x] = val[st, 0] + base

    def recv_c(st):
        for d in (1, 2, 3):
            remote(
                val.at[st, d], enter.at[st, (x + 4 - d) % 4],
                es_sem.at[st, 2, d - 1], er_sem.at[st, 2, d - 1], at_x(d),
            ).wait_recv()

    def rows(ch):
        return pl.ds(pl.multiple_of(ch * CH, CH), CH)

    def rev_states(h, carry):
        load(3, h).wait()
        load(0, h).wait()
        total = jnp.zeros((128, 128), F32)
        for ch in range(NCH):
            gt = split(io[3, h, ch * CH : (ch + 1) * CH].T)
            part = mm_nn(gt, split(io[0, h, ch * CH : (ch + 1) * CH]))
            rev_c[h, ch] = part
            total = total + part
        tot[0, h] = total
        return carry

    def fwd_states(h, carry):
        load(2, h).wait()
        load(1, h).wait()
        total = jnp.zeros((128, 128), F32)
        for ch in range(NCH):
            vtr = split(io[2, h, ch * CH : (ch + 1) * CH].T)
            part = mm_nn(vtr, split(io[1, h, ch * CH : (ch + 1) * CH]))
            fwd_c[h, ch] = part
            total = total + part
        tot[1, h] = total
        return carry

    row_at = lax.broadcasted_iota(jnp.int32, (CH, CH), 0)
    col_at = lax.broadcasted_iota(jnp.int32, (CH, CH), 1)

    causal = col_at <= row_at

    def value_part(i, carry):
        h, ch = i // NCH, i % NCH
        qk = mm_nt(split(io[0, h, rows(ch)]), split(io[1, h, rows(ch)]))
        vt[c * HEADS + h, :, rows(ch)] = mm3(split(io[3, h, rows(ch)].T), split(jnp.where(causal, qk, 0.0)))
        return carry

    def other_part(i, carry):
        h, ch = i // NCH, i % NCH
        q, k, v, g = (split(io[n, h, rows(ch)]) for n in range(4))
        gv = split(jnp.where(causal, mm_nt(g, v), 0.0))
        qg[h, rows(ch)] = mm_nn(gv, k)
        vg = split(jnp.where(row_at <= col_at, mm_nt(v, g), 0.0))
        kg[h, rows(ch)] = mm_nn(vg, q)
        return carry

    def other_parts(low, high):
        lax.fori_loop(low * NCH, high * NCH, other_part, 0)

    def vt_copy(h):
        at = c * HEADS + h
        return remote(vt.at[at], vt.at[at], vs_sem.at[h], vr_sem.at[h], sibling)

    def finish_values(h, carry):
        suffix = enter[0, h]
        at = c * HEADS + h
        for ch in reversed(range(NCH)):
            span = pl.ds(ch * CH, CH)
            more = mm_nt(split(suffix), split(io[1, h, span]))
            done = ATTN_SCALE * (vt[at, :, span] + more)
            vt[at, :, span] = done
            hi, lo = split(done)
            vthi[at, :, span] = hi
            vtlo[at, :, span] = lo
            suffix = suffix + rev_c[h, ch]
        vt_copy(h).start()
        return carry


    def out_copy(n, h):
        dst = (qg_hbm, kg_hbm)[n]
        return pltpu.make_async_copy((qg, kg)[n].at[h], dst.at[:, pl.ds(h * 128, 128)], out_sem.at[n, h])

    def finish_keys(h):
        suffix = enter[0, h]
        for ch in reversed(range(NCH)):
            span = pl.ds(ch * CH, CH)
            kg[h, span] = ATTN_SCALE * (kg[h, span] + mm_state(split(io[2, h, span]), split(suffix)))
            suffix = suffix + rev_c[h, ch]

    def finish_queries(h):
        prefix = enter[1, h]
        for ch in range(NCH):
            span = pl.ds(ch * CH, CH)
            qg[h, span] = ATTN_SCALE * (qg[h, span] + mm_state(split(io[3, h, span]), split(prefix)))
            prefix = prefix + fwd_c[h, ch]

    def finish_rest(h, carry):
        finish_keys(h)
        finish_queries(h)
        out_copy(0, h).start()
        out_copy(1, h).start()
        return carry


    def take_values(h, carry):
        at = (1 - c) * HEADS + h
        remote(vt.at[at], vt.at[at], vs_sem.at[h], vr_sem.at[h], sibling).wait_recv()
        hi, lo = split(vt[at])
        vthi[at] = hi
        vtlo[at] = lo
        return carry


    def product(p, toks=(0, 1)):
        slot, part = STEPS[p]
        span = pl.ds(toks[0] * (TOK // 2), len(toks) * (TOK // 2))

        def cut(t, carry):
            both = [xbuf[slot, rows(t), cols(half, part)] for half in (0, 1)]
            hi, lo = split(jnp.concatenate(both, axis=1))
            xhi[rows(t)] = hi
            xlo[rows(t)] = lo
            return carry

        lax.fori_loop(2 * toks[0], 2 * toks[-1] + 2, cut, 0)

        def block(a, carry):
            left = tuple(part[pl.ds(4 * a, 4), :, span].reshape(512, -1) for part in (vthi, vtlo))
            out = mm3(left, (xhi[span], xlo[span]))
            for b in (0, 1):
                near = out[b * 256 : (b + 1) * 256, :PART].reshape(4, 64, PART)
                at = 2 * a + b
                if toks[0] == 0:
                    pbuf[2 * p, at] = near
                else:
                    pbuf[2 * p, at] = pbuf[2 * p, at] + near
                for r in range(4):
                    far = out[b * 256 + r * 64 : b * 256 + (r + 1) * 64, PART:]
                    if toks[0] == 0:
                        pbuf[2 * p + 1, r, at] = far
                    else:
                        pbuf[2 * p + 1, r, at] = pbuf[2 * p + 1, r, at] + far
            return carry

        lax.fori_loop(0, 2, block, 0)

    first = ((x, at_x), (z, at_z))
    second = ((z, at_z), (x, at_x))

    def rs(j, n, src, dst, dev):
        return remote(src, dst, rss_sem.at[j, n], rsr_sem.at[j, n], dev)

    def ring1(j):
        m, at = first[j % 2]
        far = (m + 2) % 4
        return (
            rs(j, 0, pbuf.at[j, far, 0:2], rs1.at[j, 0], at(1)),
            rs(j, 1, pbuf.at[j, far, 2:4], rs1.at[j, 1], at(3)),
        )

    def ring2(j):
        m, at = first[j % 2]
        return (
            rs(j, 2, pbuf.at[j, (m + 1) % 4], rs2.at[j, 0], at(1)),
            rs(j, 3, pbuf.at[j, (m + 3) % 4], rs2.at[j, 1], at(3)),
        )

    def spread(j):
        m, _ = first[j % 2]
        n, at = second[j % 2]
        return tuple(
            rs(j, 3 + d, pbuf.at[j, m, (n + d) % 4], rs3.at[j, d - 1], at(d)) for d in (1, 2, 3)
        )

    def final(j):
        slot, part = STEPS[j // 2]
        half = j % 2
        m, _ = first[half]
        n, _ = second[half]
        target = (y + SLOT_DY[slot]) % 4
        return remote(
            pbuf.at[j, m, n], wfin.at[z, :, cols(half, part)], fs_sem.at[j], fr_sem.at[z, half, part],
            (y * 4 + x, target * 2 + c),
        )

    def stage1(j):
        for copy in ring1(j):
            copy.start()

    def stage2(j):
        m, _ = first[j % 2]
        got, send = ring1(j), ring2(j)
        got[0].wait_recv()
        up = (m + 1) % 4
        pbuf[j, up, 0:2] = pbuf[j, up, 0:2] + rs1[j, 0]
        send[0].start()
        got[1].wait_recv()
        down = (m + 3) % 4
        pbuf[j, down, 2:4] = pbuf[j, down, 2:4] + rs1[j, 1]
        send[1].start()

    def stage3(j):
        m, _ = first[j % 2]
        for copy in ring2(j):
            copy.wait_recv()
        pbuf[j, m] = pbuf[j, m] + (rs2[j, 0] + rs2[j, 1])
        for copy in spread(j):
            copy.start()

    def stage4(j):
        slot, part = STEPS[j // 2]
        half = j % 2
        m, _ = first[half]
        n, _ = second[half]
        for copy in spread(j):
            copy.wait_recv()
        pbuf[j, m, n] = (pbuf[j, m, n] + rs3[j, 0]) + (rs3[j, 1] + rs3[j, 2])
        if slot == 3:

            @pl.when(z != y)
            def _():
                final(j).start()

            @pl.when(z == y)
            def _():
                wfin[z, :, cols(half, part)] = pbuf[j, m, n]
        else:
            final(j).start()

    stages = (stage1, stage2, stage3, stage4)

    def stage(k, p):
        for half in (0, 1):
            stages[k - 1](2 * p + half)

    def arrive(p, toks=(0, 1)):
        slot, part = STEPS[p]
        if slot == 3:
            if part == 0:
                x_own.wait()
        elif slot == 2:
            for tok in toks:
                for half in (0, 1):
                    x_forward(half, part, tok).wait_recv()
        else:
            x_direct(slot == 0, 1 - slot, part).wait_recv()

    lax.fori_loop(0, HEADS, rev_states, 0)
    send_a(0)
    lax.fori_loop(0, HEADS, fwd_states, 0)
    send_b(0)
    send_a(1)
    lax.fori_loop(0, HEADS * NCH, value_part, 0)
    send_c(0)
    send_b(1)
    other_parts(0, 2)
    recv_c(0)
    lax.fori_loop(0, HEADS, finish_values, 0)
    send_c(1)
    forward(0)
    lax.fori_loop(0, HEADS, take_values, 0)

    def step(p):
        arrive(p)
        product(p)
        stage(1, p)

    def finish(low, high):
        lax.fori_loop(low, high, finish_rest, 0)

    step(0)
    step(1)
    step(2)
    stage(2, 0)
    stage(2, 1)
    step(3)
    stage(3, 0)
    stage(2, 2)
    stage(3, 1)
    forward(1)
    other_parts(2, 3)
    stage(4, 0)
    stage(2, 3)
    stage(3, 2)
    other_parts(3, 4)
    stage(4, 1)
    stage(3, 3)
    step(4)
    stage(4, 2)
    step(5)
    stage(2, 4)
    stage(4, 3)
    recv_c(1)
    finish(0, 2)
    stage(2, 5)
    step(6)
    stage(3, 4)
    stage(3, 5)
    stage(2, 6)
    finish(2, 4)
    stage(4, 4)
    stage(4, 5)
    stage(3, 6)
    arrive(7, (0,))
    product(7, (0,))
    stage(4, 6)
    arrive(7, (1,))
    product(7, (1,))
    stage(1, 7)
    stage(2, 7)
    stage(3, 7)
    stage(4, 7)

    for part in range(4):
        for zs in range(4):

            @pl.when(jnp.logical_or(z != zs, z != y))
            def _(part=part, zs=zs):
                at = cols(part // 2, part % 2)
                sem = fr_sem.at[zs, part // 2, part % 2]
                remote(pbuf.at[0, 0, 0], wfin.at[zs, :, at], fs_sem.at[0], sem, sibling).wait_recv()

    w_out[...] = wfin[...].reshape(256, 512)

    for n in (0, 1):
        for h in range(HEADS):
            out_copy(n, h).wait()
    for st in (0, 1):
        for d in (1, 2, 3):
            ex_a(st, d).wait_send()
            ex_b(st, d).wait_send()
            ex_c(st, d).wait_send()
    for h in range(HEADS):
        vt_copy(h).wait_send()
    for half in (0, 1):
        for part in (0, 1):
            x_direct(True, half, part).wait_send()
            x_direct(False, half, part).wait_send()
            x_forward(half, part, 0).wait_send()
            x_forward(half, part, 1).wait_send()
    for j in range(JOBS):
        for ring in (ring1, ring2, spread):
            for copy in ring(j):
                copy.wait_send()
        if STEPS[j // 2][0] == 3:

            @pl.when(z != y)
            def _(j=j):
                final(j).wait_send()
        else:
            final(j).wait_send()


def last_kernel(qg_in, kg_in, w_in, rowst, colst, qg_out, kg_out, upd, rown, coln, stage, sem):
    pieces = [(n, i) for n in (0, 1) for i in range(4)]

    def load(n, i):
        return pltpu.make_async_copy((qg_in, kg_in)[n].at[pl.ds(i * 256, 256)], stage.at[n, i], sem.at[0, n, i])

    def store(n, i):
        return pltpu.make_async_copy(stage.at[n, i], (qg_out, kg_out)[n].at[pl.ds(i * 256, 256)], sem.at[1, n, i])

    for piece in pieces:
        load(*piece).start()
    for piece in pieces:
        load(*piece).wait()
        store(*piece).start()
    w = w_in[...] / jnp.sqrt(F32(16384.0))
    squares = w * w + MOMENT_EPS
    row_mean = jnp.broadcast_to(jnp.mean(squares, axis=1, keepdims=True), (256, 128))
    col_mean = jnp.mean(squares, axis=0, keepdims=True)
    row_old = jnp.broadcast_to(rowst[...], (128, 256)).T
    row_new = DECAY * row_old + (1.0 - DECAY) * row_mean
    col_new = DECAY * colst[...] + (1.0 - DECAY) * col_mean
    rown[...] = row_new.T[0:1]
    coln[...] = col_new
    row_one = row_new[:, 0:1]
    average = jnp.mean(row_one, axis=0, keepdims=True)
    upd[...] = w * lax.rsqrt(row_one * col_new / average)
    for piece in pieces:
        store(*piece).wait()


def shards(queries, keys, values, out_grad, inputs, row_state, col_state):
    hbm = pl.BlockSpec(memory_space=pl.ANY)
    vmem = pl.BlockSpec(memory_space=pltpu.VMEM)
    dma = pltpu.SemaphoreType.DMA
    scratch = [
        pltpu.VMEM((4, HEADS, TOK, 128), F32),
        pltpu.VMEM((HEADS, TOK, 128), F32),
        pltpu.VMEM((HEADS, TOK, 128), F32),
        pltpu.VMEM((2 * HEADS, 128, TOK), F32),
        pltpu.VMEM((2 * HEADS, 128, TOK), BF16),
        pltpu.VMEM((2 * HEADS, 128, TOK), BF16),
        pltpu.VMEM((4, TOK, 512), F32),
        pltpu.VMEM((TOK, 2 * PART), BF16),
        pltpu.VMEM((TOK, 2 * PART), BF16),
        pltpu.VMEM((HEADS, NCH, 128, 128), F32),
        pltpu.VMEM((HEADS, NCH, 128, 128), F32),
        pltpu.VMEM((2, HEADS, 128, 128), F32),
        pltpu.VMEM((2, 3, 128, 128), F32),
        pltpu.VMEM((2, 4, 128, 128), F32),
        pltpu.VMEM((2, 128, 128), F32),
        pltpu.VMEM((2, 3, 128, 128), F32),
        pltpu.VMEM((2, HEADS, 128, 128), F32),
        pltpu.VMEM((JOBS, 4, 4, 64, PART), F32),
        pltpu.VMEM((JOBS, 2, 2, 64, PART), F32),
        pltpu.VMEM((JOBS, 2, 4, 64, PART), F32),
        pltpu.VMEM((JOBS, 3, 64, PART), F32),
        pltpu.VMEM((4, 64, 512), F32),
        dma((4, HEADS)),
        dma,
        dma((2, 2, 2)),
        dma((2, 2, 2)),
        dma((2, 4)),
        dma((2, 4)),
        dma((2, 3, 3)),
        dma((2, 3, 3)),
        dma((HEADS,)),
        dma((HEADS,)),
        dma((JOBS, 7)),
        dma((JOBS, 7)),
        dma((JOBS,)),
        dma((4, 2, 2)),
        dma((2, HEADS)),
    ]
    tokens = jax.ShapeDtypeStruct((TOK, 512), F32)
    block = jax.ShapeDtypeStruct((256, 512), F32)
    query_grad, key_grad, weight_grad = pl.pallas_call(
        kernel,
        out_shape=(tokens, tokens, block),
        in_specs=[hbm] * 5,
        out_specs=(hbm, hbm, vmem),
        scratch_shapes=scratch,
        compiler_params=pltpu.CompilerParams(
            collective_id=0, has_side_effects=True, vmem_limit_bytes=60 * 1024 * 1024
        ),
        cost_estimate=pl.CostEstimate(flops=20_000_000_000, bytes_accessed=16_000_000, transcendentals=0),
    )(queries, keys, values, out_grad, inputs)
    return pl.pallas_call(
        last_kernel,
        out_shape=(
            tokens,
            tokens,
            block,
            jax.ShapeDtypeStruct((1, 256), F32),
            jax.ShapeDtypeStruct((1, 512), F32),
        ),
        in_specs=[hbm] * 2 + [vmem] * 3,
        out_specs=(hbm, hbm, vmem, vmem, vmem),
        scratch_shapes=[pltpu.VMEM((2, 4, 256, 512), F32), dma((2, 2, 4))],
        compiler_params=pltpu.CompilerParams(vmem_limit_bytes=60 * 1024 * 1024),
        cost_estimate=pl.CostEstimate(flops=2_000_000, bytes_accessed=10_000_000, transcendentals=131072),
    )(query_grad, key_grad, weight_grad, row_state, col_state)


def solution(mesh):
    in_specs = (
        P("seq", "head"),
        P("seq", "head"),
        P("seq", "head"),
        P("seq", "head"),
        P("seq", "head"),
        P("head", "seq"),
        P("seq", "head"),
    )
    out_specs = (
        P("seq", "head"),
        P("seq", "head"),
        P("seq", "head"),
        P("head", "seq"),
        P("seq", "head"),
    )
    return jax.shard_map(shards, mesh=mesh, in_specs=in_specs, out_specs=out_specs, check_vma=False)
```

time: 126 us -> 121 us (0.960); the launches traced: 124 us -> 121 us
  local copies, waits for them, and re-layouts: 6.54 us -> 0 us
  Pallas kernels: 117 us -> 120 us
    unnamed x13 -> x0, local copies, waits for them, and re-layouts: 6.54 us -> none
    pallas_call x1 -> x2, Pallas kernels: 117 us -> 120 us  [the longest x1 114 us: shards(): pl.pallas_call(kernel, out_shape=(tokens, tokens, block), in_specs=[hbm]...]
where the time goes in v1:
time: 121 us
  Pallas kernels  120 us (99%)
    pallas_call x1, Pallas kernels, shards(): pl.pallas_call(kernel, out_shape=(tokens, tokens, block), in_specs=[hbm]...  114 us
    pallas_call x1, Pallas kernels, shards(): pl.pallas_call(last_kernel, out_shape=(tokens, tokens, block, jax.ShapeDt...  5.44 us

profile of v1, /device:TPU:104, one launch (start us, length us, event | category | flops | bytes accessed | tf_op | source)
XLA Modules:
  0.0 120.7 jit_solution(3440832613193969025)
XLA Ops:
  0.6 114.4 %shard_map.110 = (f32[1024,512]{1,0:T(8,128)}, f32[1024,512]{1,0:T(8,128)}, f32[256,512]{1,0:T(8,128)}) custom-call(f32[1024,512]{1,0:T(8,128)} %q_hbm.1, f32[1024,512]{1,0:T(8,128)} %k_hbm.1, f32[1024,512]{1,0:T(8,128)} %v_hbm.1, f32[1024,512]{1,0:T(8,128)} %g_hbm.1, f32[1024,512]{1,0:T(8,128)} %x_hbm.1), custom_call_target="tpu_custom_call" | custom-call | flops 20000000000 | bytes 16000000 | tf_op jit(solution)/shard_map/pallas_call | solution.py:623
  115.1 5.4 %shard_map.111 = (f32[1024,512]{1,0:T(8,128)}, f32[1024,512]{1,0:T(8,128)}, f32[256,512]{1,0:T(8,128)}, f32[1,256]{1,0:T(1,128)}, f32[1,512]{1,0:T(1,128)}) custom-call(f32[1024,512]{1,0:T(8,128)} %get-tuple-element.8.qg_in, f32[1024,512]{1,0:T(8,128)} %get-tuple-element.9.kg_in, f32[256,512]{1,0:T(8,128)} %get-tuple-element.10.w_in, f32[1,256]{1,0:T(1,128)} %rowst.1, ...), custom_call_target="tpu_custom_call" | custom-call | flops 2000000 | bytes 10000000 | tf_op jit(solution)/shard_map/pallas_call | solution.py:634

commit v2 on v1

--- a/solution.py
+++ b/solution.py
@@ -26,6 +26,7 @@
 SLOT_DY = (3, 1, 2, 0)
 STEPS = ((3, 0), (3, 1), (0, 0), (1, 0), (0, 1), (1, 1), (2, 0), (2, 1))
 JOBS = 2 * len(STEPS)
+RINGED = 6
 
 
 def dot(a, b, dims=NN):
@@ -64,9 +65,9 @@
 def kernel(
     q_hbm, k_hbm, v_hbm, g_hbm, x_hbm,
     qg_hbm, kg_hbm, w_out,
-    io, qg, kg, vt, vthi, vtlo, xbuf, xhi, xlo,
+    io, qg, kg, vt, vtc, xbuf, xc,
     rev_c, fwd_c, tot, ex1, val, tz, ex2, enter,
-    pbuf, rs1, rs2, rs3, wfin,
+    pbuf, rs1, rs2, rs3, rs4, wfin,
     ld_sem, xo_sem, xs_sem, xr_sem, xf_sem, xg_sem, es_sem, er_sem, vs_sem, vr_sem,
     rss_sem, rsr_sem, fs_sem, fr_sem, out_sem,
 ):
@@ -75,14 +76,22 @@
     z, x = sq // 4, sq % 4
     y, c = hd // 2, hd % 2
 
+    x_at = [x] + [(x + d) % 4 for d in (1, 2, 3)]
+    z_at = [z] + [(z + d) % 4 for d in (1, 2, 3)]
+    y_at = [y] + [(y + d) % 4 for d in (1, 2, 3)]
+    x_ids = [z * 4 + x_at[d] for d in range(4)]
+    z_ids = [z_at[d] * 4 + x for d in range(4)]
+    y_ids = [y_at[d] * 2 + c for d in range(4)]
+    last_seq = y * 4 + x
+
     def at_x(d):
-        return (z * 4 + (x + d) % 4, hd)
+        return (x_ids[d], hd)
 
     def at_z(d):
-        return (((z + d) % 4) * 4 + x, hd)
+        return (z_ids[d], hd)
 
     def at_y(d):
-        return (sq, ((y + d) % 4) * 2 + c)
+        return (sq, y_ids[d])
 
     sibling = (sq, y * 2 + 1 - c)
 
@@ -263,8 +272,9 @@
             done = ATTN_SCALE * (vt[at, :, span] + more)
             vt[at, :, span] = done
             hi, lo = split(done)
-            vthi[at, :, span] = hi
-            vtlo[at, :, span] = lo
+            vtc[at, :, span] = hi
+            vtc[at, :, pl.ds(TOK + ch * CH, CH)] = lo
+            vtc[at, :, pl.ds(2 * TOK + ch * CH, CH)] = hi
             suffix = suffix + rev_c[h, ch]
         vt_copy(h).start()
         return carry
@@ -300,27 +310,33 @@
         at = (1 - c) * HEADS + h
         remote(vt.at[at], vt.at[at], vs_sem.at[h], vr_sem.at[h], sibling).wait_recv()
         hi, lo = split(vt[at])
-        vthi[at] = hi
-        vtlo[at] = lo
+        vtc[at, :, 0:TOK] = hi
+        vtc[at, :, TOK : 2 * TOK] = lo
+        vtc[at, :, 2 * TOK : 3 * TOK] = hi
         return carry
 
 
     def product(p, toks=(0, 1)):
         slot, part = STEPS[p]
-        span = pl.ds(toks[0] * (TOK // 2), len(toks) * (TOK // 2))
 
         def cut(t, carry):
             both = [xbuf[slot, rows(t), cols(half, part)] for half in (0, 1)]
             hi, lo = split(jnp.concatenate(both, axis=1))
-            xhi[rows(t)] = hi
-            xlo[rows(t)] = lo
+            xc[rows(t)] = hi
+            xc[rows(t + NCH)] = hi
+            xc[rows(t + 2 * NCH)] = lo
             return carry
 
         lax.fori_loop(2 * toks[0], 2 * toks[-1] + 2, cut, 0)
 
         def block(a, carry):
-            left = tuple(part[pl.ds(4 * a, 4), :, span].reshape(512, -1) for part in (vthi, vtlo))
-            out = mm3(left, (xhi[span], xlo[span]))
+            blocks = pl.ds(4 * a, 4)
+            if len(toks) == 2:
+                out = dot(vtc[blocks].reshape(512, 3 * TOK), xc[...])
+            else:
+                low = toks[0] * (TOK // 2)
+                spans = [pl.ds(low + n * TOK, TOK // 2) for n in range(3)]
+                out = sum(dot(vtc[blocks, :, span].reshape(512, TOK // 2), xc[span]) for span in spans)
             for b in (0, 1):
                 near = out[b * 256 : (b + 1) * 256, :PART].reshape(4, 64, PART)
                 at = 2 * a + b
@@ -338,15 +354,15 @@
 
         lax.fori_loop(0, 2, block, 0)
 
-    first = ((x, at_x), (z, at_z))
-    second = ((z, at_z), (x, at_x))
+    first = ((x_at, at_x), (z_at, at_z))
+    second = ((z_at, at_z), (x_at, at_x))
 
     def rs(j, n, src, dst, dev):
         return remote(src, dst, rss_sem.at[j, n], rsr_sem.at[j, n], dev)
 
     def ring1(j):
         m, at = first[j % 2]
-        far = (m + 2) % 4
+        far = m[2]
         return (
             rs(j, 0, pbuf.at[j, far, 0:2], rs1.at[j, 0], at(1)),
             rs(j, 1, pbuf.at[j, far, 2:4], rs1.at[j, 1], at(3)),
@@ -355,15 +371,34 @@
     def ring2(j):
         m, at = first[j % 2]
         return (
-            rs(j, 2, pbuf.at[j, (m + 1) % 4], rs2.at[j, 0], at(1)),
-            rs(j, 3, pbuf.at[j, (m + 3) % 4], rs2.at[j, 1], at(3)),
-        )
+            rs(j, 2, pbuf.at[j, m[1]], rs2.at[j, 0], at(1)),
+            rs(j, 3, pbuf.at[j, m[3]], rs2.at[j, 1], at(3)),
+        )
+
+    def ring3(j):
+        m, _ = first[j % 2]
+        n, at = second[j % 2]
+        return (
+            rs(j, 4, pbuf.at[j, m[0], n[2], 0:32], rs3.at[j, 0, 0:32], at(1)),
+            rs(j, 5, pbuf.at[j, m[0], n[2], 32:64], rs3.at[j, 1, 0:32], at(3)),
+        )
+
+    def ring4(j):
+        m, _ = first[j % 2]
+        n, at = second[j % 2]
+        return (
+            rs(j, 6, pbuf.at[j, m[0], n[1]], rs4.at[j, 0], at(1)),
+            rs(j, 7, pbuf.at[j, m[0], n[3]], rs4.at[j, 1], at(3)),
+        )
+
+    def ringed(j):
+        return j // 2 < RINGED
 
     def spread(j):
         m, _ = first[j % 2]
         n, at = second[j % 2]
         return tuple(
-            rs(j, 3 + d, pbuf.at[j, m, (n + d) % 4], rs3.at[j, d - 1], at(d)) for d in (1, 2, 3)
+            rs(j, 3 + d, pbuf.at[j, m[0], n[d]], rs3.at[j, d - 1], at(d)) for d in (1, 2, 3)
         )
 
     def final(j):
@@ -371,10 +406,9 @@
         half = j % 2
         m, _ = first[half]
         n, _ = second[half]
-        target = (y + SLOT_DY[slot]) % 4
         return remote(
-            pbuf.at[j, m, n], wfin.at[z, :, cols(half, part)], fs_sem.at[j], fr_sem.at[z, half, part],
-            (y * 4 + x, target * 2 + c),
+            pbuf.at[j, m[0], n[0]], wfin.at[z, :, cols(half, part)], fs_sem.at[j], fr_sem.at[z, half, part],
+            (last_seq, y_ids[SLOT_DY[slot]]),
         )
 
     def stage1(j):
@@ -385,11 +419,11 @@
         m, _ = first[j % 2]
         got, send = ring1(j), ring2(j)
         got[0].wait_recv()
-        up = (m + 1) % 4
+        up = m[1]
         pbuf[j, up, 0:2] = pbuf[j, up, 0:2] + rs1[j, 0]
         send[0].start()
         got[1].wait_recv()
-        down = (m + 3) % 4
+        down = m[3]
         pbuf[j, down, 2:4] = pbuf[j, down, 2:4] + rs1[j, 1]
         send[1].start()
 
@@ -397,18 +431,34 @@
         m, _ = first[j % 2]
         for copy in ring2(j):
             copy.wait_recv()
-        pbuf[j, m] = pbuf[j, m] + (rs2[j, 0] + rs2[j, 1])
-        for copy in spread(j):
+        pbuf[j, m[0]] = pbuf[j, m[0]] + (rs2[j, 0] + rs2[j, 1])
+        for copy in ring3(j) if ringed(j) else spread(j):
             copy.start()
 
     def stage4(j):
+        m, _ = first[j % 2]
+        n, _ = second[j % 2]
+        got, send = ring3(j), ring4(j)
+        got[0].wait_recv()
+        pbuf[j, m[0], n[1], 0:32] = pbuf[j, m[0], n[1], 0:32] + rs3[j, 0, 0:32]
+        send[0].start()
+        got[1].wait_recv()
+        pbuf[j, m[0], n[3], 32:64] = pbuf[j, m[0], n[3], 32:64] + rs3[j, 1, 0:32]
+        send[1].start()
+
+    def stage5(j):
         slot, part = STEPS[j // 2]
         half = j % 2
         m, _ = first[half]
         n, _ = second[half]
-        for copy in spread(j):
-            copy.wait_recv()
-        pbuf[j, m, n] = (pbuf[j, m, n] + rs3[j, 0]) + (rs3[j, 1] + rs3[j, 2])
+        if ringed(j):
+            for copy in ring4(j):
+                copy.wait_recv()
+            pbuf[j, m[0], n[0]] = pbuf[j, m[0], n[0]] + (rs4[j, 0] + rs4[j, 1])
+        else:
+            for copy in spread(j):
+                copy.wait_recv()
+            pbuf[j, m[0], n[0]] = (pbuf[j, m[0], n[0]] + rs3[j, 0]) + (rs3[j, 1] + rs3[j, 2])
         if slot == 3:
 
             @pl.when(z != y)
@@ -417,11 +467,11 @@
 
             @pl.when(z == y)
             def _():
-                wfin[z, :, cols(half, part)] = pbuf[j, m, n]
+                wfin[z, :, cols(half, part)] = pbuf[j, m[0], n[0]]
         else:
             final(j).start()
 
-    stages = (stage1, stage2, stage3, stage4)
+    stages = (stage1, stage2, stage3, stage4, stage5)
 
     def stage(k, p):
         for half in (0, 1):
@@ -443,14 +493,13 @@
     send_a(0)
     lax.fori_loop(0, HEADS, fwd_states, 0)
     send_b(0)
-    send_a(1)
     lax.fori_loop(0, HEADS * NCH, value_part, 0)
     send_c(0)
-    send_b(1)
+    send_a(1)
     other_parts(0, 2)
     recv_c(0)
     lax.fori_loop(0, HEADS, finish_values, 0)
-    send_c(1)
+    send_b(1)
     forward(0)
     lax.fori_loop(0, HEADS, take_values, 0)
 
@@ -463,6 +512,7 @@
         lax.fori_loop(low, high, finish_rest, 0)
 
     step(0)
+    send_c(1)
     step(1)
     step(2)
     stage(2, 0)
@@ -476,34 +526,40 @@
     stage(4, 0)
     stage(2, 3)
     stage(3, 2)
+    stage(4, 1)
     other_parts(3, 4)
-    stage(4, 1)
+    stage(5, 0)
     stage(3, 3)
+    stage(4, 2)
+    stage(5, 1)
     step(4)
-    stage(4, 2)
+    stage(4, 3)
+    stage(5, 2)
     step(5)
     stage(2, 4)
-    stage(4, 3)
+    stage(5, 3)
     recv_c(1)
     finish(0, 2)
     stage(2, 5)
+    stage(3, 4)
     step(6)
-    stage(3, 4)
     stage(3, 5)
+    stage(4, 4)
     stage(2, 6)
     finish(2, 4)
-    stage(4, 4)
     stage(4, 5)
+    stage(5, 4)
     stage(3, 6)
     arrive(7, (0,))
     product(7, (0,))
-    stage(4, 6)
+    stage(5, 5)
     arrive(7, (1,))
     product(7, (1,))
     stage(1, 7)
+    stage(5, 6)
     stage(2, 7)
     stage(3, 7)
-    stage(4, 7)
+    stage(5, 7)
 
     for part in range(4):
         for zs in range(4):
@@ -533,7 +589,7 @@
             x_forward(half, part, 0).wait_send()
             x_forward(half, part, 1).wait_send()
     for j in range(JOBS):
-        for ring in (ring1, ring2, spread):
+        for ring in (ring1, ring2, ring3, ring4) if ringed(j) else (ring1, ring2, spread):
             for copy in ring(j):
                 copy.wait_send()
         if STEPS[j // 2][0] == 3:
@@ -545,7 +601,9 @@
             final(j).wait_send()
 
 
-def last_kernel(qg_in, kg_in, w_in, rowst, colst, qg_out, kg_out, upd, rown, coln, stage, sem):
+def last_kernel(qg_in, kg_in, w_in, rowst, colst, qg_out, kg_out, upd, rown, coln, stage, wbuf, sem, w_sem):
+    w_load = pltpu.make_async_copy(w_in, wbuf, w_sem)
+    w_load.start()
     pieces = [(n, i) for n in (0, 1) for i in range(4)]
 
     def load(n, i):
@@ -559,7 +617,8 @@
     for piece in pieces:
         load(*piece).wait()
         store(*piece).start()
-    w = w_in[...] / jnp.sqrt(F32(16384.0))
+    w_load.wait()
+    w = wbuf[...] / jnp.sqrt(F32(16384.0))
     squares = w * w + MOMENT_EPS
     row_mean = jnp.broadcast_to(jnp.mean(squares, axis=1, keepdims=True), (256, 128))
     col_mean = jnp.mean(squares, axis=0, keepdims=True)
@@ -584,11 +643,9 @@
         pltpu.VMEM((HEADS, TOK, 128), F32),
         pltpu.VMEM((HEADS, TOK, 128), F32),
         pltpu.VMEM((2 * HEADS, 128, TOK), F32),
-        pltpu.VMEM((2 * HEADS, 128, TOK), BF16),
-        pltpu.VMEM((2 * HEADS, 128, TOK), BF16),
+        pltpu.VMEM((2 * HEADS, 128, 3 * TOK), BF16),
         pltpu.VMEM((4, TOK, 512), F32),
-        pltpu.VMEM((TOK, 2 * PART), BF16),
-        pltpu.VMEM((TOK, 2 * PART), BF16),
+        pltpu.VMEM((3 * TOK, 2 * PART), BF16),
         pltpu.VMEM((HEADS, NCH, 128, 128), F32),
         pltpu.VMEM((HEADS, NCH, 128, 128), F32),
         pltpu.VMEM((2, HEADS, 128, 128), F32),
@@ -601,6 +658,7 @@
         pltpu.VMEM((JOBS, 2, 2, 64, PART), F32),
         pltpu.VMEM((JOBS, 2, 4, 64, PART), F32),
         pltpu.VMEM((JOBS, 3, 64, PART), F32),
+        pltpu.VMEM((JOBS, 2, 64, PART), F32),
         pltpu.VMEM((4, 64, 512), F32),
         dma((4, HEADS)),
         dma,
@@ -612,8 +670,8 @@
         dma((2, 3, 3)),
         dma((HEADS,)),
         dma((HEADS,)),
-        dma((JOBS, 7)),
-        dma((JOBS, 7)),
+        dma((JOBS, 8)),
+        dma((JOBS, 8)),
         dma((JOBS,)),
         dma((4, 2, 2)),
         dma((2, HEADS)),
@@ -640,9 +698,9 @@
             jax.ShapeDtypeStruct((1, 256), F32),
             jax.ShapeDtypeStruct((1, 512), F32),
         ),
-        in_specs=[hbm] * 2 + [vmem] * 3,
+        in_specs=[hbm] * 3 + [vmem] * 2,
         out_specs=(hbm, hbm, vmem, vmem, vmem),
-        scratch_shapes=[pltpu.VMEM((2, 4, 256, 512), F32), dma((2, 2, 4))],
+        scratch_shapes=[pltpu.VMEM((2, 4, 256, 512), F32), pltpu.VMEM((256, 512), F32), dma((2, 2, 4)), dma],
         compiler_params=pltpu.CompilerParams(vmem_limit_bytes=60 * 1024 * 1024),
         cost_estimate=pl.CostEstimate(flops=2_000_000, bytes_accessed=10_000_000, transcendentals=131072),
     )(query_grad, key_grad, weight_grad, row_state, col_state)

time: 121 us -> 118 us (0.975)
  Pallas kernels: 120 us -> 116 us
    pallas_call x1, Pallas kernels: 114 us -> 110 us  [shards(): pl.pallas_call(kernel, out_shape=(tokens, tokens, block), in_specs=[hbm]...]
where the time goes in v2:
time: 118 us; the launch traced here: 117 us
  Pallas kernels  116 us (98%)
    pallas_call x1, Pallas kernels, shards(): pl.pallas_call(kernel, out_shape=(tokens, tokens, block), in_specs=[hbm]...  110 us
    pallas_call x1, Pallas kernels, shards(): pl.pallas_call(last_kernel, out_shape=(tokens, tokens, block, jax.ShapeDt...  5.64 us

profile of v2, /device:TPU:104, one launch (start us, length us, event | category | flops | bytes accessed | tf_op | source)
XLA Modules:
  0.0 116.8 jit_solution(11396056340812694910)
XLA Ops:
  0.6 110.3 %shard_map.110 = (f32[1024,512]{1,0:T(8,128)}, f32[1024,512]{1,0:T(8,128)}, f32[256,512]{1,0:T(8,128)}) custom-call(f32[1024,512]{1,0:T(8,128)} %q_hbm.1, f32[1024,512]{1,0:T(8,128)} %k_hbm.1, f32[1024,512]{1,0:T(8,128)} %v_hbm.1, f32[1024,512]{1,0:T(8,128)} %g_hbm.1, f32[1024,512]{1,0:T(8,128)} %x_hbm.1), custom_call_target="tpu_custom_call" | custom-call | flops 20000000000 | bytes 16000000 | tf_op jit(solution)/shard_map/pallas_call | solution.py:681
  111.0 5.6 %shard_map.111 = (f32[1024,512]{1,0:T(8,128)}, f32[1024,512]{1,0:T(8,128)}, f32[256,512]{1,0:T(8,128)}, f32[1,256]{1,0:T(1,128)}, f32[1,512]{1,0:T(1,128)}) custom-call(f32[1024,512]{1,0:T(8,128)} %get-tuple-element.8.qg_in, f32[1024,512]{1,0:T(8,128)} %get-tuple-element.9.kg_in, f32[256,512]{1,0:T(8,128)} %get-tuple-element.10.w_in, f32[1,256]{1,0:T(1,128)} %rowst.1, ...), custom_call_target="tpu_custom_call" | custom-call | flops 2000000 | bytes 10000000 | tf_op jit(solution)/shard_map/pallas_call | solution.py:692

commit v3 on v2

--- a/solution.py
+++ b/solution.py
@@ -514,21 +514,21 @@
     step(0)
     send_c(1)
     step(1)
+    stage(2, 0)
     step(2)
-    stage(2, 0)
     stage(2, 1)
+    stage(3, 0)
     step(3)
-    stage(3, 0)
     stage(2, 2)
     stage(3, 1)
+    stage(4, 0)
     forward(1)
     other_parts(2, 3)
-    stage(4, 0)
     stage(2, 3)
     stage(3, 2)
     stage(4, 1)
+    stage(5, 0)
     other_parts(3, 4)
-    stage(5, 0)
     stage(3, 3)
     stage(4, 2)
     stage(5, 1)
@@ -614,7 +614,7 @@
 
     for piece in pieces:
         load(*piece).start()
-    for piece in pieces:
+    for piece in pieces[:4]:
         load(*piece).wait()
         store(*piece).start()
     w_load.wait()
@@ -629,6 +629,9 @@
     coln[...] = col_new
     row_one = row_new[:, 0:1]
     average = jnp.mean(row_one, axis=0, keepdims=True)
+    for piece in pieces[4:]:
+        load(*piece).wait()
+        store(*piece).start()
     upd[...] = w * lax.rsqrt(row_one * col_new / average)
     for piece in pieces:
         store(*piece).wait()

time: 118 us -> 118 us (level)
  no operation moved by 1% of the time
where the time goes in v3:
time: 118 us; the launch traced here: 117 us
  Pallas kernels  116 us (98%)
    pallas_call x1, Pallas kernels, shards(): pl.pallas_call(kernel, out_shape=(tokens, tokens, block), in_specs=[hbm]...  110 us
    pallas_call x1, Pallas kernels, shards(): pl.pallas_call(last_kernel, out_shape=(tokens, tokens, block, jax.ShapeDt...  5.85 us

profile of v3, /device:TPU:104, one launch (start us, length us, event | category | flops | bytes accessed | tf_op | source)
XLA Modules:
  0.0 116.8 jit_solution(14631730753981043019)
XLA Ops:
  0.6 110.1 %shard_map.110 = (f32[1024,512]{1,0:T(8,128)}, f32[1024,512]{1,0:T(8,128)}, f32[256,512]{1,0:T(8,128)}) custom-call(f32[1024,512]{1,0:T(8,128)} %q_hbm.1, f32[1024,512]{1,0:T(8,128)} %k_hbm.1, f32[1024,512]{1,0:T(8,128)} %v_hbm.1, f32[1024,512]{1,0:T(8,128)} %g_hbm.1, f32[1024,512]{1,0:T(8,128)} %x_hbm.1), custom_call_target="tpu_custom_call" | custom-call | flops 20000000000 | bytes 16000000 | tf_op jit(solution)/shard_map/pallas_call | solution.py:684
  110.8 5.9 %shard_map.111 = (f32[1024,512]{1,0:T(8,128)}, f32[1024,512]{1,0:T(8,128)}, f32[256,512]{1,0:T(8,128)}, f32[1,256]{1,0:T(1,128)}, f32[1,512]{1,0:T(1,128)}) custom-call(f32[1024,512]{1,0:T(8,128)} %get-tuple-element.8.qg_in, f32[1024,512]{1,0:T(8,128)} %get-tuple-element.9.kg_in, f32[256,512]{1,0:T(8,128)} %get-tuple-element.10.w_in, f32[1,256]{1,0:T(1,128)} %rowst.1, ...), custom_call_target="tpu_custom_call" | custom-call | flops 2000000 | bytes 10000000 | tf_op jit(solution)/shard_map/pallas_call | solution.py:695

commit v4 on v3

--- a/solution.py
+++ b/solution.py
@@ -178,7 +178,7 @@
         return reached.astype(F32)
 
     def send_a(st):
-        for d in (1, 2, 3):
+        for d in (2, 1, 3):
             ex_a(st, d).start()
 
     def send_b(st):
@@ -186,7 +186,7 @@
             ex_a(st, d).wait_recv()
         parts = [tot[st, x]] + [ex1[st, d - 1] for d in (1, 2, 3)]
         tz[st] = parts[0] + parts[1] + parts[2] + parts[3]
-        for d in (1, 2, 3):
+        for d in (2, 1, 3):
             ex_b(st, d).start()
         for e in range(4):
             target = (x + e) % 4
@@ -197,7 +197,7 @@
         for d in (1, 2, 3):
             ex_b(st, d).wait_recv()
         base = sum(counts(st, (z + 4 - d) % 4, z) * ex2[st, d - 1] for d in (1, 2, 3))
-        for e in (1, 2, 3):
+        for e in (2, 1, 3):
             val[st, e] = val[st, e] + base
             ex_c(st, e).start()
         enter[st, x] = val[st, 0] + base
@@ -316,7 +316,7 @@
         return carry
 
 
-    def product(p, toks=(0, 1)):
+    def product(p, toks=(0, 1), between=None):
         slot, part = STEPS[p]
 
         def cut(t, carry):
@@ -352,7 +352,12 @@
                         pbuf[2 * p + 1, r, at] = pbuf[2 * p + 1, r, at] + far
             return carry
 
-        lax.fori_loop(0, 2, block, 0)
+        if between is None:
+            lax.fori_loop(0, 2, block, 0)
+        else:
+            block(c, 0)
+            between()
+            block(1 - c, 0)
 
     first = ((x_at, at_x), (z_at, at_z))
     second = ((z_at, at_z), (x_at, at_x))
@@ -501,7 +506,6 @@
     lax.fori_loop(0, HEADS, finish_values, 0)
     send_b(1)
     forward(0)
-    lax.fori_loop(0, HEADS, take_values, 0)
 
     def step(p):
         arrive(p)
@@ -511,7 +515,9 @@
     def finish(low, high):
         lax.fori_loop(low, high, finish_rest, 0)
 
-    step(0)
+    arrive(0)
+    product(0, between=lambda: lax.fori_loop(0, HEADS, take_values, 0))
+    stage(1, 0)
     send_c(1)
     step(1)
     stage(2, 0)
@@ -614,7 +620,7 @@
 
     for piece in pieces:
         load(*piece).start()
-    for piece in pieces[:4]:
+    for piece in pieces:
         load(*piece).wait()
         store(*piece).start()
     w_load.wait()
@@ -629,9 +635,6 @@
     coln[...] = col_new
     row_one = row_new[:, 0:1]
     average = jnp.mean(row_one, axis=0, keepdims=True)
-    for piece in pieces[4:]:
-        load(*piece).wait()
-        store(*piece).start()
     upd[...] = w * lax.rsqrt(row_one * col_new / average)
     for piece in pieces:
         store(*piece).wait()

time: 118 us -> 117 us (level)
  no operation moved by 1% of the time
where the time goes in v4:
time: 117 us
  Pallas kernels  116 us (99%)
    pallas_call x1, Pallas kernels, shards(): pl.pallas_call(kernel, out_shape=(tokens, tokens, block), in_specs=[hbm]...  110 us
    pallas_call x1, Pallas kernels, shards(): pl.pallas_call(last_kernel, out_shape=(tokens, tokens, block, jax.ShapeDt...  5.64 us

profile of v4, /device:TPU:104, one launch (start us, length us, event | category | flops | bytes accessed | tf_op | source)
XLA Modules:
  0.0 116.7 jit_solution(14202315023117185269)
XLA Ops:
  0.6 110.2 %shard_map.110 = (f32[1024,512]{1,0:T(8,128)}, f32[1024,512]{1,0:T(8,128)}, f32[256,512]{1,0:T(8,128)}) custom-call(f32[1024,512]{1,0:T(8,128)} %q_hbm.1, f32[1024,512]{1,0:T(8,128)} %k_hbm.1, f32[1024,512]{1,0:T(8,128)} %v_hbm.1, f32[1024,512]{1,0:T(8,128)} %g_hbm.1, f32[1024,512]{1,0:T(8,128)} %x_hbm.1), custom_call_target="tpu_custom_call" | custom-call | flops 20000000000 | bytes 16000000 | tf_op jit(solution)/shard_map/pallas_call | solution.py:687
  110.9 5.6 %shard_map.111 = (f32[1024,512]{1,0:T(8,128)}, f32[1024,512]{1,0:T(8,128)}, f32[256,512]{1,0:T(8,128)}, f32[1,256]{1,0:T(1,128)}, f32[1,512]{1,0:T(1,128)}) custom-call(f32[1024,512]{1,0:T(8,128)} %get-tuple-element.8.qg_in, f32[1024,512]{1,0:T(8,128)} %get-tuple-element.9.kg_in, f32[256,512]{1,0:T(8,128)} %get-tuple-element.10.w_in, f32[1,256]{1,0:T(1,128)} %rowst.1, ...), custom_call_target="tpu_custom_call" | custom-call | flops 2000000 | bytes 10000000 | tf_op jit(solution)/shard_map/pallas_call | solution.py:698
